TPU v7x, 512 devices: a whole 4x4x16 slice. The times are simulated.
512 devices in a mesh: term: 8 (over y, core), sector: 64 (over x, z).
Axes of the slice: x: 4, y: 4, z: 16, core: 2. Of those that a mesh axis runs over, the one named last changes fastest.
Arguments:
- vectors: bfloat16 [3, 256, 256, 256], P(None, 'sector'), may hold values from -128 to 128
- dims: int32 [256, 2], P('sector'), may hold values from 64 to 256, as said below
- offsets: int32 [32], P('term'), may hold values from -2 to 2, as said below
- left_env: bfloat16 [32, 256, 256, 256], P('term', 'sector'), may hold values from -0.0625 to 0.0625
- right_env: bfloat16 [32, 256, 256, 256], P('term', 'sector'), may hold values from -0.375 to 0.375
Outputs:
- products: bfloat16 [3, 256, 256, 256], P(None, 'sector', 'term')
- subspace: float32 [3, 3], replicated
Inputs may be any that keep to these rules, and one draw needn't show every extreme that they name: `dims`: each sector block has at most 256 rows and columns; some sector has exactly 256 of both. `offsets`: some term has offset -2 and some term +2.
All inputs are finite; a program needn't handle non-finite values.
Results may differ from a plain program's by a relative error of at most 0.011.
Values may be sent and summed in bfloat16 or wider, within the bound.
A program may use at most 64 MiB of HBM per device.

v0:
```python
import jax
import jax.numpy as jnp
from jax import lax
from jax.sharding import PartitionSpec as P

REACH = 2


def extended(value, sides, width):
    for axis, dim in sides:
        size, length = (lax.axis_size(axis), value.shape[dim])
        up = [(i, (i + 1) % size) for i in range(size - 1)]
        down = [(j, i) for i, j in up]
        last = lax.slice_in_dim(value, length - width, length, axis=dim)
        initial = lax.slice_in_dim(value, 0, width, axis=dim)
        before = lax.ppermute(last, axis, up)
        after = lax.ppermute(initial, axis, down)
        value = jnp.concatenate([before, value, after], axis=dim)
    return value


def block_mask(dims, size):
    rows = jnp.arange(size, dtype=jnp.int32)
    return (rows[None, :, None] < dims[:, 0][:, None, None]) & (
        rows[None, None, :] < dims[:, 1][:, None, None]
    )


def body(vectors, dims, offsets, left_env, right_env):
    sec_here = vectors.shape[1]
    width = vectors.shape[2]
    mask = block_mask(dims, width)
    psi = jnp.where(mask[None], vectors, jnp.zeros_like(vectors))
    padded = extended(psi, (("sector", 1),), REACH)
    slabs = jnp.stack(
        [
            lax.dynamic_slice_in_dim(padded, REACH - offsets[j], sec_here, 1)
            for j in range(offsets.shape[0])
        ]
    )
    inner = jnp.einsum(
        "tvsab,tscb->tvsac", slabs, right_env, preferred_element_type=jnp.float32
    ).astype(jnp.bfloat16)
    partial_sum = jnp.einsum(
        "tsda,tvsac->vsdc", left_env, inner, preferred_element_type=jnp.float32
    )
    row_count = width // lax.axis_size("term")
    first_row = lax.axis_index("term") * row_count
    summed = lax.psum(partial_sum, "term")
    mine = lax.dynamic_slice_in_dim(summed, first_row, row_count, 2)
    psi_rows = lax.dynamic_slice_in_dim(psi, first_row, row_count, 2)
    mask_rows = lax.dynamic_slice_in_dim(mask, first_row, row_count, 1)
    correlation = jnp.einsum("isab,jsab->ij", psi_rows.astype(jnp.float32), mine)
    subspace = lax.psum(correlation, ("term", "sector"))
    products = jnp.where(mask_rows[None], mine, jnp.zeros_like(mine)).astype(jnp.bfloat16)
    return (products, subspace)


def solution(mesh):
    return jax.shard_map(
        body,
        mesh=mesh,
        in_specs=(
            P(None, "sector", None, None),
            P("sector", None),
            P("term"),
            P("term", "sector", None, None),
            P("term", "sector", None, None),
        ),
        out_specs=(P(None, "sector", "term", None), P()),
        check_vma=False,
    )
```

profile of v0, /device:TPU:1, one launch (start us, length us, event | category | flops | bytes accessed | tf_op | source)
XLA Modules:
  0.0 237.6 jit_solution(3847647677643665452)
XLA Ops:
  0.6 0.8 slice_bitcast_fusion.1
  1.8 0.4 copy.12
  2.2 3.5 %copy_select_fusion = bf16[3,4,256,256]{3,0,1,2:T(4,128)(2,1)S(1)} fusion(bf16[3,4,256,256]{3,2,1,0:T(8,128)(2,1)} %param.5, pred[4,256,256]{2,0,1:T(4,128)(4,1)S(1)} %copy.12), kind=kLoop, calls=%fused_computation.9 | loop fusion | flops 786432 | bytes 3407872 | tf_op jit(solution)/shard_map/jit(_where)/select_n | solution.py:33
  5.7 0.7 fusion.23
  6.5 0.7 copy-done.1
  7.3 1.3 collective-permute-start.1
  8.6 1.1 copy.14
  9.7 5.9 %collective-permute-start = (bf16[3,2,256,256]{3,2,1,0:T(8,128)(2,1)}, bf16[3,2,256,256]{3,2,1,0:T(8,128)(2,1)}, u32[]{:S(2)}, u32[]{:S(2)}) collective-permute-start(bf16[3,2,256,256]{3,2,1,0:T(8,128)(2,1)} %copy.14), channel_id=1, source_target_pairs={{0,1},{1,2},{2,3},{3,4},{4,5},{5,6},{6,7},{7,8},{8,9},{9,10},{10,1... | collective-permute-start | bytes 2359304 | tf_op jit(solution)/shard_map/ppermute | solution.py:16
  15.6 0.7 fusion.24
  21.6 0.2 constant_dynamic-slice_fusion.1
  21.8 1.8 collective-permute-done.1
  23.5 1.8 copy.17
  25.3 0.4 collective-permute-done
  25.7 1.8 copy.16
  27.5 3.0 %pad_maximum_fusion.1 = bf16[3,8,256,256]{3,0,1,2:T(4,128)(2,1)S(1)} fusion(bf16[3,2,256,256]{3,0,1,2:T(4,128)(2,1)S(1)} %copy.17, bf16[3,4,256,256]{3,0,1,2:T(4,128)(2,1)S(1)} %copy-done.2, bf16[3,2,256,256]{3,0,1,2:T(4,128)(2,1)S(1)} %copy.16), kind=kLoop, calls=%fused_computation.6 | loop fusion | flops 3145728 | bytes 6291456 | tf_op jit(solution)/shard_map/concatenate | solution.py:18
  30.5 4.3 %dynamic-slice_bitcast_fusion.3 = (bf16[1,3,4,256,256]{4,1,2,3,0:T(4,128)(2,1)S(1)}, bf16[1,3,4,256,256]{4,1,2,3,0:T(4,128)(2,1)S(1)}, bf16[1,3,4,256,256]{4,1,2...) fusion(bf16[3,8,256,256]{3,0,1,2:T(4,128)(2,1)S(1)} %pad_maximum_fusion.1, s32[]{:T(128)S(6)} %select_n.27, ...), kind=kLoop, calls=%fused_computation.13 | loop fusion | bytes 12582928 | tf_op jit(solution)/shard_map/stack | solution.py:35
  34.8 8.8 %pad_maximum_fusion = bf16[4,3,4,256,256]{4,1,2,3,0:T(4,128)(2,1)} fusion(bf16[1,3,4,256,256]{4,1,2,3,0:T(4,128)(2,1)S(1)} %get-tuple-element.9, bf16[1,3,4,256,256]{4,1,2,3,0:T(4,128)(2,1)S(1)} %get-tuple-element.10, bf16[1,3,4,256,256]{4,1,2,3,0:T(4,128)(2,1)S(1)} %get-tuple-element.11, bf16[1,3,4,256,256]{4,1,2,3,0:T(4,128)(2,1)S(1)} %get-tuple-element.8), kind=kLoop, calls=%fused_computation | loop fusion | flops 9437184 | bytes 12582912 | tf_op jit(solution)/shard_map/stack | solution.py:35
  43.6 11.4 %fusion.12 = f32[3,4,256,256]{2,3,0,1:T(8,128)} fusion(bf16[4,3,4,256,256]{4,1,2,3,0:T(4,128)(2,1)} %pad_maximum_fusion, bf16[4,4,256,256]{3,2,1,0:T(8,128)(2,1)S(1)} %copy-done, bf16[4,4,256,256]{3,2,1,0:T(8,128)(2,1)} %param.9), kind=kOutput, calls=%fused_computation.14 | convolution fusion | flops 3224371200 | bytes 13631488 | tf_op jit(solution)/shard_map/tsda,tvsac->vsdc/dot_general | solution.py:44
  55.0 61.2 %all-reduce.1 = bf16[3,4,256,256]{2,3,0,1:T(8,128)(2,1)} all-reduce(f32[3,4,256,256]{2,3,0,1:T(8,128)} %fusion.12), channel_id=1, replica_groups=mesh['term'=8,'sector'=64] {'term'}, use_global_device_ids=true, to_apply=%region_0.1 | all-reduce | flops 786432 | bytes 4718592 | tf_op jit(solution)/shard_map/psum | solution.py:49
  116.2 2.5 %select_convert_fusion = (bf16[3,4,32,256]{2,3,0,1:T(8,128)(2,1)S(1)}, bf16[3,4,32,256]{2,3,0,1:T(8,128)(2,1)}) fusion(pred[4,32,256]{1,2,0:T(8,128)(4,1)S(1)} %constant_dynamic-slice_fusion.1, bf16[3,4,256,256]{2,3,0,1:T(8,128)(2,1)} %all-reduce.1, s32[]{:T(128)S(6)} %select_n.25), kind=kLoop, calls=%fused_computation.15 | loop fusion | flops 98304 | bytes 622596 | tf_op jit(solution)/shard_map/convert_element_type | solution.py:55
  118.7 1.6 copy.19
  120.3 1.4 convolution_bitcast_fusion
  121.7 0.9 copy.20
  122.7 115.0 %psum.15 = f32[3,3]{1,0:T(4,128)} all-reduce(f32[3,3]{1,0:T(4,128)S(1)} %convolution_bitcast_fusion), channel_id=1, replica_groups=mesh['term'=8,'sector'=64] {'term','sector'}, use_global_device_ids=true, to_apply=%region_1.2 | all-reduce | flops 9 | bytes 72 | tf_op jit(solution)/shard_map/psum | solution.py:54
  (10 shorter events, 0.5 us)
Async XLA Ops:
  0.6 43.0 %copy-start = (bf16[4,4,256,256]{3,2,1,0:T(8,128)(2,1)S(1)}, bf16[4,4,256,256]{3,2,1,0:T(8,128)(2,1)}, u32[]{:S(2)}) copy-start(bf16[4,4,256,256]{3,2,1,0:T(8,128)(2,1)} %param.8) | copy-start | bytes 6291460
  5.7 1.4 copy-start.1
  7.2 8.5 %copy-start.3 = (s32[4]{0:T(128)S(1)}, s32[4]{0:T(128)}, u32[]{:S(2)}) copy-start(s32[4]{0:T(128)} %param.7) | copy-start | bytes 52
  7.3 16.2 %collective-permute-start.1 = (bf16[3,2,256,256]{3,2,1,0:T(8,128)(2,1)S(1)}, bf16[3,2,256,256]{3,2,1,0:T(8,128)(2,1)}, u32[]{:S(2)}, u32[]{:S(2)}) collective-permute-start(bf16[3,2,256,256]{3,2,1,0:T(8,128)(2,1)S(1)} %copy.15), channel_id=1, source_target_pairs={{1,0},{2,1},{3,2},{4,3},{5,4},{6,5},{7,6},{8,7},{9,8},{10,9},{11,1... | collective-permute-start | bytes 2359304 | tf_op jit(solution)/shard_map/ppermute | solution.py:17
  9.7 16.0 %collective-permute-start = (bf16[3,2,256,256]{3,2,1,0:T(8,128)(2,1)}, bf16[3,2,256,256]{3,2,1,0:T(8,128)(2,1)}, u32[]{:S(2)}, u32[]{:S(2)}) collective-permute-start(bf16[3,2,256,256]{3,2,1,0:T(8,128)(2,1)} %copy.14), channel_id=1, source_target_pairs={{0,1},{1,2},{2,3},{3,4},{4,5},{5,6},{6,7},{7,8},{8,9},{9,10},{10,1... | collective-permute-start | bytes 2359304 | tf_op jit(solution)/shard_map/ppermute | solution.py:16
  21.5 6.0 %copy-start.2 = (bf16[3,4,256,256]{3,0,1,2:T(4,128)(2,1)S(1)}, bf16[3,4,256,256]{3,0,1,2:T(4,128)(2,1)}, u32[]{:S(2)}) copy-start(bf16[3,4,256,256]{3,0,1,2:T(4,128)(2,1)} %copy-done.1) | copy-start | bytes 4718596
where the time goes:
time: 238 us
  blocking collectives  176 us (74%)
  other arithmetic  18.1 us (8%)
  local copies, waits for them, and re-layouts  15.3 us (6%)
  matrix products  12.8 us (5%)
  starting transfers between devices  7.18 us (3%)
  between operations  6 us (3%)
    psum x1, blocking collectives, body(): subspace = lax.psum(correlation, ('term', 'sector'))  115 us
    psum x1, blocking collectives, body(): summed = lax.psum(partial_sum, 'term')  61.2 us
    dot_general x1, matrix products, body(): jnp.einsum('tsda,tvsac->vsdc', left_env, inner, preferred_element_type=jn...  11.4 us
    another operation x1, other arithmetic, body(): jnp.stack([lax.dynamic_slice_in_dim(padded, REACH - offsets[j], sec_here,...  8.82 us
    ppermute x1, starting transfers between devices, extended(): before = lax.ppermute(last, axis, up)  5.89 us
  transfers between devices with their start and end apart: 2, of which 2 were waited for; matrix products, arithmetic and copies ran while one was open for 2% of the time, Pallas kernels for 0%

commit v1 on v0

v1 whole, which is shorter than its diff:
```python
import jax
import jax.numpy as jnp
from jax import lax
from jax.experimental import pallas as pl
from jax.experimental.pallas import tpu as pltpu
from jax.sharding import PartitionSpec as P

MESH = pl.DeviceIdType.MESH
NV = 3
F32 = jnp.float32
BF16 = jnp.bfloat16


def dot_nt(a, b):
    return lax.dot_general(a, b, (((1,), (1,)), ((), ())), preferred_element_type=F32)


def make_kernel(nz, nx):
    nsec = nz * nx

    def kernel(dims, offsets, vectors, lenv, renv, prod, sub,
               ext0, ext1, ext2, part0, part1, part2, lbuf, rbuf,
               sibrx, ysrc, yrx, ar1, ar2, ar3,
               vec_sem, env_sem, zs_sem, zr_sem, fs_sem, fr_sem, ss_sem, sr_sem, ys_sem, yr_sem,
               as_sem, a_sem, relay):
        ext = (ext0, ext1, ext2)
        part = (part0, part1, part2)
        k = lax.axis_index("term")
        g = lax.axis_index("sector")
        y = k // 2
        c = lax.rem(k, 2)
        sib = k + 1 - 2 * c
        zbase = (g // nz) * nz
        zi = lax.rem(g, nz)

        def zpeer(d):
            return zbase + lax.rem(zi + d + nz, nz)

        def ypeer(d):
            return lax.rem(k + 2 * d + 8, 8)

        def term_peer(d):
            return lax.rem(k + d, 8)

        def x_peer(d):
            return lax.rem(g + nz * d, nsec)

        nxt = lax.rem(g + 1, nsec)
        prv = lax.rem(g + nsec - 1, nsec)

        def dev(kk, gg):
            return {"term": kk, "sector": gg}

        def remote(src, dst, s_sem, r_sem, kk, gg):
            return pltpu.make_async_remote_copy(
                src_ref=src, dst_ref=dst, send_sem=s_sem, recv_sem=r_sem,
                device_id=dev(kk, gg), device_id_type=MESH)

        vec_cp = [pltpu.make_async_copy(vectors.at[v], ext[v].at[pl.ds(2, 4)], vec_sem.at[v])
                  for v in range(NV)]
        for cp in vec_cp:
            cp.start()
        renv_cp = pltpu.make_async_copy(renv, rbuf, env_sem.at[0])
        lenv_cp = pltpu.make_async_copy(lenv, lbuf, env_sem.at[1])
        renv_cp.start()
        lenv_cp.start()

        barrier = pltpu.get_barrier_semaphore()
        near = ([(term_peer(d), g) for d in range(1, 8)] + [(k, nxt), (k, prv), (k, zpeer(1)), (k, zpeer(-1))]
                + [(k, x_peer(d)) for d in range(1, nx)])
        for p in near:
            pl.semaphore_signal(barrier, inc=1, device_id=dev(*p), device_id_type=MESH)

        masks = []
        row_id = lax.broadcasted_iota(jnp.int32, (256, 256), 0)
        col_id = lax.broadcasted_iota(jnp.int32, (256, 256), 1)
        for s in range(4):
            inside = (row_id < dims[0, s]) & (col_id < dims[1, s])
            masks.append(jnp.where(inside, 1.0, 0.0).astype(BF16))
        for v in range(NV):
            vec_cp[v].wait()
            for s in range(4):
                ext[v][2 + s] = ext[v][2 + s] * masks[s]
        pl.semaphore_wait(barrier, len(near))

        up, down = [], []
        for v in range(NV):
            a = remote(ext[v].at[4 + c], ext[v].at[c], zs_sem.at[v, 0], zr_sem.at[v, 0], k, nxt)
            b = remote(ext[v].at[2 + c], ext[v].at[6 + c], zs_sem.at[v, 1], zr_sem.at[v, 1], k, prv)
            a.start()
            b.start()
            up.append(a)
            down.append(b)

        def tell(step, dist):
            for d in (dist, -dist):
                pl.semaphore_signal(relay.at[step], inc=1, device_id=dev(k, zpeer(d)), device_id_type=MESH)

        def hear(step):
            pl.semaphore_wait(relay.at[step], 2)

        tell(0, 1)

        sib_cp, y_cp = [], []

        def sib_send(v):
            cp = remote(part[v].at[:, :, 1 - c], sibrx.at[v], ss_sem.at[v], sr_sem.at[v], sib, g)
            cp.start()
            sib_cp.append(cp)

        def chip_sum(v):
            sib_cp[v].wait()
            for yy in range(4):
                for s in range(4):
                    both = part[v][s, yy, c].astype(F32) + sibrx[v, s, yy].astype(F32)
                    ysrc[v, yy, s] = both.astype(BF16)
            for d in (2, 1, 3):
                dest = lax.rem(y + d, 4)
                cp = remote(ysrc.at[v, dest], yrx.at[v, d - 1], ys_sem.at[v, d - 1], yr_sem.at[v, d - 1],
                            ypeer(d), g)
                cp.start()
                y_cp.append(cp)

        accs = {}
        for v in range(NV):
            if v >= 1:
                chip_sum(v - 1)
            up[v].wait_recv()
            down[v].wait_recv()
            fa = remote(ext[v].at[c], ext[v].at[c], fs_sem.at[v, 0], fr_sem.at[v, 0], sib, g)
            fb = remote(ext[v].at[6 + c], ext[v].at[6 + c], fs_sem.at[v, 1], fr_sem.at[v, 1], sib, g)
            fa.start()
            fb.start()
            fa.wait()
            fb.wait()

            @pl.when(g == 0)
            def _():
                ext[v][0:2] = jnp.zeros((2, 256, 256), BF16)

            @pl.when(g == nsec - 1)
            def _():
                ext[v][6:8] = jnp.zeros((2, 256, 256), BF16)

            if v == 0:
                renv_cp.wait()
                lenv_cp.wait()
            for s in range(4):
                tot = None
                for t in range(4):
                    inner = dot_nt(ext[v][2 + s - offsets[t]], rbuf[t, s]).astype(BF16)
                    term = jnp.dot(lbuf[t, s], inner, preferred_element_type=F32)
                    tot = term if tot is None else tot + term
                part[v][s] = tot.reshape(4, 2, 32, 256).astype(BF16)
                for i in range(NV):
                    z = ext[i][2 + s].astype(F32) * tot
                    z = jnp.sum(z.reshape(32, 8, 256), axis=0)
                    z = z[:, :128] + z[:, 128:]
                    accs[i, v] = z if s == 0 else accs[i, v] + z
            sib_send(v)
            if v < 2:
                hear(v)
                tell(v + 1, 2 * (v + 1))

        rows = jnp.concatenate(
            [jnp.sum(accs[i, j], axis=0, keepdims=True) for i in range(NV) for j in range(NV)], axis=0)
        sums = jnp.sum(rows, axis=1, keepdims=True)
        diag = (lax.broadcasted_iota(jnp.int32, (9, 128), 0)
                == lax.broadcasted_iota(jnp.int32, (9, 128), 1))
        ar1[0] = jnp.sum(jnp.where(diag, sums, 0.0), axis=0, keepdims=True)

        def spread(buf, n, sem, peer):
            cps = [remote(buf.at[0], buf.at[d], as_sem.at[sem], a_sem.at[sem], *peer(d)) for d in range(1, n)]
            for cp in cps:
                cp.start()

        def gather(buf, n, sem):
            pltpu.make_async_copy(buf.at[pl.ds(1, n - 1)], buf.at[pl.ds(1, n - 1)], a_sem.at[sem]).wait()
            return jnp.sum(buf[...], axis=0)

        def drain(buf, n, sem):
            pltpu.make_async_copy(buf.at[pl.ds(1, n - 1)], buf.at[pl.ds(1, n - 1)], as_sem.at[sem]).wait()

        spread(ar1, 8, 0, lambda d: (term_peer(d), g))
        chip_sum(2)
        ar2[0] = gather(ar1, 8, 0)
        spread(ar2, nx, 1, lambda d: (k, x_peer(d)))
        ar3[0] = gather(ar2, nx, 1)
        hear(2)
        spread(ar3, nz, 2, lambda d: (k, zpeer(d)))

        lane = lax.broadcasted_iota(jnp.int32, (32, 256), 1)
        rown = lax.broadcasted_iota(jnp.int32, (32, 256), 0) + k * 32
        for v in range(NV):
            for j in range(3):
                y_cp[3 * v + j].wait()
            for s in range(4):
                tot = ysrc[v, y, s].astype(F32)
                for d in range(3):
                    tot = tot + yrx[v, d, s].astype(F32)
                inside = (rown < dims[0, s]) & (lane < dims[1, s])
                prod[v, s] = jnp.where(inside, tot, 0.0).astype(BF16)
        for v in range(NV):
            up[v].wait_send()
            down[v].wait_send()
        drain(ar1, 8, 0)
        drain(ar2, nx, 1)
        drain(ar3, nz, 2)
        sub[...] = gather(ar3, nz, 2)

    return kernel


def solution(mesh):
    nz = 16
    nx = mesh.shape["sector"] // nz
    vmem = pl.BlockSpec(memory_space=pltpu.VMEM)
    smem = pl.BlockSpec(memory_space=pltpu.SMEM)
    hbm = pl.BlockSpec(memory_space=pl.ANY)
    dma = pltpu.SemaphoreType.DMA

    def body(vectors, dims, offsets, left_env, right_env):
        prod, row = pl.pallas_call(
            make_kernel(nz, nx),
            out_shape=(jax.ShapeDtypeStruct((NV, 4, 32, 256), BF16),
                       jax.ShapeDtypeStruct((1, 128), F32)),
            in_specs=[smem, smem, hbm, hbm, hbm],
            out_specs=(vmem, vmem),
            scratch_shapes=(
                [pltpu.VMEM((8, 256, 256), BF16)] * 3
                + [pltpu.VMEM((4, 4, 2, 32, 256), BF16)] * 3
                + [pltpu.VMEM((4, 4, 256, 256), BF16)] * 2
                + [pltpu.VMEM((NV, 4, 4, 32, 256), BF16),
                   pltpu.VMEM((NV, 4, 4, 32, 256), BF16),
                   pltpu.VMEM((NV, 3, 4, 32, 256), BF16),
                   pltpu.VMEM((8, 1, 128), F32),
                   pltpu.VMEM((nx, 1, 128), F32),
                   pltpu.VMEM((nz, 1, 128), F32),
                   dma((NV,)), dma((2,)), dma((NV, 2)), dma((NV, 2)), dma((NV, 2)), dma((NV, 2)),
                   dma((NV,)), dma((NV,)), dma((NV, 3)), dma((NV, 3)),
                   dma((3,)), dma((3,)), pltpu.SemaphoreType.REGULAR((3,))]),
            compiler_params=pltpu.CompilerParams(
                collective_id=0, has_side_effects=True, vmem_limit_bytes=56 << 20),
        )(dims.T, offsets, vectors, left_env, right_env)
        return prod, row[0, :9].reshape(3, 3)

    return jax.shard_map(
        body,
        mesh=mesh,
        in_specs=(
            P(None, "sector", None, None),
            P("sector", None),
            P("term"),
            P("term", "sector", None, None),
            P("term", "sector", None, None),
        ),
        out_specs=(P(None, "sector", "term", None), P()),
        check_vma=False,
    )
```

time: 238 us -> 49.3 us (0.21)
  blocking collectives: 176 us -> 0 us
  Pallas kernels: 0 us -> 45.5 us
  other arithmetic: 18.1 us -> 0 us
  matrix products: 12.8 us -> 0 us
  local copies, waits for them, and re-layouts: 15.3 us -> 2.96 us
  starting transfers between devices: 7.18 us -> 0 us
  between operations: 6 us -> 0.64 us
    psum x2 -> x0, blocking collectives: 176 us -> none  [the longest x1 115 us: body(): subspace = lax.psum(correlation, ('term', 'sector'))]
    pallas_call x0 -> x1, Pallas kernels: none -> 45.5 us  [body(): pl.pallas_call(make_kernel(nz, nx), out_shape=(jax.ShapeDtypeStruct((NV,...]
    dot_general x2 -> x0, matrix products: 12.8 us -> none  [the longest x1 11.4 us: body(): jnp.einsum('tsda,tvsac->vsdc', left_env, inner, preferred_element_type=jn...]
    another operation x1 -> x0, other arithmetic: 8.82 us -> none  [body(): jnp.stack([lax.dynamic_slice_in_dim(padded, REACH - offsets[j], sec_here,...]
    ppermute x2 -> x0, starting transfers between devices: 7.18 us -> none  [the longest x1 5.89 us: extended(): before = lax.ppermute(last, axis, up)]
    ppermute x2 -> x0, local copies, waits for them, and re-layouts: 3.62 us -> none  [the longest x1 1.81 us: extended(): after = lax.ppermute(initial, axis, down)]
    another operation x1, local copies, waits for them, and re-layouts: 4.26 us -> 0.66 us  [body(): return (prod, row[0, :9].reshape(3, 3))]
    select_n x1 -> x0, other arithmetic: 3.49 us -> none  [body(): psi = jnp.where(mask[None], vectors, jnp.zeros_like(vectors))]
  transfers between devices with their start and end apart: 2 -> 0, of which waited for: 2 -> 0; matrix products, arithmetic and copies ran while one was open for 2% -> 0% of each run, Pallas kernels for 0% -> 0%
where the time goes in v1:
time: 49.3 us; the launch traced here: 49.1 us
  Pallas kernels  45.5 us (92%)
  local copies, waits for them, and re-layouts  2.96 us (6%)
  between operations  0.64 us (1%)
    pallas_call x1, Pallas kernels, body(): pl.pallas_call(make_kernel(nz, nx), out_shape=(jax.ShapeDtypeStruct((NV,...  45.5 us
    unnamed x1, local copies, waits for them, and re-layouts  1.62 us

profile of v1, /device:TPU:1, one launch (start us, length us, event | category | flops | bytes accessed | tf_op | source)
XLA Modules:
  0.0 49.1 jit_solution(620278360662172457)
XLA Ops:
  0.6 45.5 %shard_map.68 = (bf16[3,4,32,256]{3,2,1,0:T(8,128)(2,1)}, f32[1,128]{1,0:T(1,128)}) custom-call(s32[2,4]{1,0:T(2,128)} %bitcast.1, s32[4]{0:T(128)} %offsets.1, bf16[3,4,256,256]{3,2,1,0:T(8,128)(2,1)} %vectors.1, bf16[4,4,256,256]{3,2,1,0:T(8,128)(2,1)} %lenv.1, bf16[4,4,256,256]{3,2,1,0:T(8,128)(2,1)} %renv.1), custom_call_target="tpu_custom_call" | custom-call | tf_op jit(solution)/shard_map/pallas_call | solution.py:223
  46.1 0.7 %slice_reduce_fusion = f32[9]{0:T(128)S(1)} fusion(f32[1,128]{1,0:T(1,128)} %get-tuple-element.5), kind=kLoop, calls=%fused_computation | loop fusion | bytes 72 | tf_op jit(solution)/shard_map/slice | solution.py:245
  46.8 0.7 %reshape_squeeze.3 = f32[3,3]{1,0:T(4,128)} reshape(f32[9]{0:T(128)S(1)} %slice_reduce_fusion) | data formatting | bytes 72 | tf_op jit(solution)/shard_map/reshape;squeeze | solution.py:245
  47.5 1.6 %copy.8 = bf16[3,4,32,256]{3,2,1,0:T(8,128)(2,1)} copy(bf16[3,4,32,256]{3,2,1,0:T(8,128)(2,1)} %get-tuple-element.8) | data formatting | bytes 393216

commit v2 on v1

--- a/solution.py
+++ b/solution.py
@@ -18,10 +18,10 @@
 def make_kernel(nz, nx):
     nsec = nz * nx
 
-    def kernel(dims, offsets, vectors, lenv, renv, prod, sub,
+    def kernel(dims_hbm, offsets_hbm, vectors, lenv, renv, prod, sub,
                ext0, ext1, ext2, part0, part1, part2, lbuf, rbuf,
-               sibrx, ysrc, yrx, ar1, ar2, ar3,
-               vec_sem, env_sem, zs_sem, zr_sem, fs_sem, fr_sem, ss_sem, sr_sem, ys_sem, yr_sem,
+               sibrx, ysrc, yrx, ar1, ar3, dims, offsets,
+               vec_sem, env_sem, int_sem, zs_sem, zr_sem, fs_sem, fr_sem, ss_sem, sr_sem, ys_sem, yr_sem,
                as_sem, a_sem, relay):
         ext = (ext0, ext1, ext2)
         part = (part0, part1, part2)
@@ -56,6 +56,17 @@
                 src_ref=src, dst_ref=dst, send_sem=s_sem, recv_sem=r_sem,
                 device_id=dev(kk, gg), device_id_type=MESH)
 
+        barrier = pltpu.get_barrier_semaphore()
+        beside = [(sib, g), (ypeer(1), g), (ypeer(-1), g), (k, x_peer(1)), (k, x_peer(nx - 1)),
+                  (k, zpeer(1)), (k, zpeer(-1))]
+        near = beside + [(k, nxt), (k, prv)]
+        for p in near:
+            pl.semaphore_signal(barrier, inc=1, device_id=dev(*p), device_id_type=MESH)
+
+        dims_cp = pltpu.make_async_copy(dims_hbm, dims, int_sem.at[0])
+        offs_cp = pltpu.make_async_copy(offsets_hbm, offsets, int_sem.at[1])
+        dims_cp.start()
+        offs_cp.start()
         vec_cp = [pltpu.make_async_copy(vectors.at[v], ext[v].at[pl.ds(2, 4)], vec_sem.at[v])
                   for v in range(NV)]
         for cp in vec_cp:
@@ -65,12 +76,8 @@
         renv_cp.start()
         lenv_cp.start()
 
-        barrier = pltpu.get_barrier_semaphore()
-        near = ([(term_peer(d), g) for d in range(1, 8)] + [(k, nxt), (k, prv), (k, zpeer(1)), (k, zpeer(-1))]
-                + [(k, x_peer(d)) for d in range(1, nx)])
-        for p in near:
-            pl.semaphore_signal(barrier, inc=1, device_id=dev(*p), device_id_type=MESH)
-
+        dims_cp.wait()
+        offs_cp.wait()
         masks = []
         row_id = lax.broadcasted_iota(jnp.int32, (256, 256), 0)
         col_id = lax.broadcasted_iota(jnp.int32, (256, 256), 1)
@@ -92,14 +99,18 @@
             up.append(a)
             down.append(b)
 
-        def tell(step, dist):
-            for d in (dist, -dist):
-                pl.semaphore_signal(relay.at[step], inc=1, device_id=dev(k, zpeer(d)), device_id_type=MESH)
+        chain = [beside,
+                 [(sib, g), (ypeer(2), g), (k, x_peer(2)), (k, zpeer(2)), (k, zpeer(-2))],
+                 [(ypeer(2), g), (k, zpeer(4)), (k, zpeer(-4))]]
+
+        def tell(step):
+            for p in chain[step]:
+                pl.semaphore_signal(relay.at[step], inc=1, device_id=dev(*p), device_id_type=MESH)
 
         def hear(step):
-            pl.semaphore_wait(relay.at[step], 2)
-
-        tell(0, 1)
+            pl.semaphore_wait(relay.at[step], len(chain[step]))
+
+        tell(0)
 
         sib_cp, y_cp = [], []
 
@@ -125,6 +136,9 @@
         for v in range(NV):
             if v >= 1:
                 chip_sum(v - 1)
+            if v == 0:
+                hear(0)
+                tell(1)
             up[v].wait_recv()
             down[v].wait_recv()
             fa = remote(ext[v].at[c], ext[v].at[c], fs_sem.at[v, 0], fr_sem.at[v, 0], sib, g)
@@ -158,9 +172,9 @@
                     z = z[:, :128] + z[:, 128:]
                     accs[i, v] = z if s == 0 else accs[i, v] + z
             sib_send(v)
-            if v < 2:
-                hear(v)
-                tell(v + 1, 2 * (v + 1))
+            if v == 0:
+                hear(1)
+                tell(2)
 
         rows = jnp.concatenate(
             [jnp.sum(accs[i, j], axis=0, keepdims=True) for i in range(NV) for j in range(NV)], axis=0)
@@ -169,25 +183,23 @@
                 == lax.broadcasted_iota(jnp.int32, (9, 128), 1))
         ar1[0] = jnp.sum(jnp.where(diag, sums, 0.0), axis=0, keepdims=True)
 
-        def spread(buf, n, sem, peer):
-            cps = [remote(buf.at[0], buf.at[d], as_sem.at[sem], a_sem.at[sem], *peer(d)) for d in range(1, n)]
-            for cp in cps:
-                cp.start()
-
-        def gather(buf, n, sem):
-            pltpu.make_async_copy(buf.at[pl.ds(1, n - 1)], buf.at[pl.ds(1, n - 1)], a_sem.at[sem]).wait()
-            return jnp.sum(buf[...], axis=0)
-
-        def drain(buf, n, sem):
-            pltpu.make_async_copy(buf.at[pl.ds(1, n - 1)], buf.at[pl.ds(1, n - 1)], as_sem.at[sem]).wait()
-
-        spread(ar1, 8, 0, lambda d: (term_peer(d), g))
+        def spread(buf, sem, peers):
+            for d, peer in peers:
+                remote(buf.at[0], buf.at[d], as_sem.at[sem], a_sem.at[sem], *peer).start()
+
+        def others(buf, sem):
+            n = buf.shape[0] - 1
+            return pltpu.make_async_copy(buf.at[pl.ds(1, n)], buf.at[pl.ds(1, n)], sem)
+
+        hear(2)
+        plane = sorted(((dx, dk) for dx in range(nx) for dk in range(8) if dx + dk),
+                       key=lambda p: -(min(p[0], nx - p[0]) + min(p[1] // 2, 4 - p[1] // 2)))
+        spread(ar1, 0, [(8 * dx + dk, (term_peer(dk), x_peer(dx))) for dx, dk in plane])
         chip_sum(2)
-        ar2[0] = gather(ar1, 8, 0)
-        spread(ar2, nx, 1, lambda d: (k, x_peer(d)))
-        ar3[0] = gather(ar2, nx, 1)
-        hear(2)
-        spread(ar3, nz, 2, lambda d: (k, zpeer(d)))
+        others(ar1, a_sem.at[0]).wait()
+        ar3[0] = jnp.sum(ar1[...], axis=0)
+        line = sorted(range(1, nz), key=lambda d: -min(d, nz - d))
+        spread(ar3, 1, [(d, (k, zpeer(d))) for d in line])
 
         lane = lax.broadcasted_iota(jnp.int32, (32, 256), 1)
         rown = lax.broadcasted_iota(jnp.int32, (32, 256), 0) + k * 32
@@ -203,28 +215,38 @@
         for v in range(NV):
             up[v].wait_send()
             down[v].wait_send()
-        drain(ar1, 8, 0)
-        drain(ar2, nx, 1)
-        drain(ar3, nz, 2)
-        sub[...] = gather(ar3, nz, 2)
+        others(ar1, as_sem.at[0]).wait()
+        others(ar3, as_sem.at[1]).wait()
+        others(ar3, a_sem.at[1]).wait()
+        sums = jnp.broadcast_to(jnp.sum(ar3[...], axis=0), (3, 128))
+        r3 = lax.broadcasted_iota(jnp.int32, (3, 128), 0)
+        l3 = lax.broadcasted_iota(jnp.int32, (3, 128), 1)
+        full = jnp.zeros((3, 128), F32)
+        for j in range(NV):
+            col = jnp.sum(jnp.where(l3 == 3 * r3 + j, sums, 0.0), axis=1, keepdims=True)
+            full = jnp.where(l3 == j, col, full)
+        sub[...] = full[:, :3]
 
     return kernel
+
+
+def hand_over(prod_in, sub_in, prod, sub):
+    prod[...] = prod_in[...]
+    sub[...] = sub_in[...]
 
 
 def solution(mesh):
     nz = 16
     nx = mesh.shape["sector"] // nz
     vmem = pl.BlockSpec(memory_space=pltpu.VMEM)
-    smem = pl.BlockSpec(memory_space=pltpu.SMEM)
     hbm = pl.BlockSpec(memory_space=pl.ANY)
     dma = pltpu.SemaphoreType.DMA
 
     def body(vectors, dims, offsets, left_env, right_env):
-        prod, row = pl.pallas_call(
+        prod, sub = pl.pallas_call(
             make_kernel(nz, nx),
-            out_shape=(jax.ShapeDtypeStruct((NV, 4, 32, 256), BF16),
-                       jax.ShapeDtypeStruct((1, 128), F32)),
-            in_specs=[smem, smem, hbm, hbm, hbm],
+            out_shape=(pltpu.VMEM((NV, 4, 32, 256), BF16), pltpu.VMEM((3, 3), F32)),
+            in_specs=[hbm] * 5,
             out_specs=(vmem, vmem),
             scratch_shapes=(
                 [pltpu.VMEM((8, 256, 256), BF16)] * 3
@@ -233,16 +255,23 @@
                 + [pltpu.VMEM((NV, 4, 4, 32, 256), BF16),
                    pltpu.VMEM((NV, 4, 4, 32, 256), BF16),
                    pltpu.VMEM((NV, 3, 4, 32, 256), BF16),
-                   pltpu.VMEM((8, 1, 128), F32),
-                   pltpu.VMEM((nx, 1, 128), F32),
+                   pltpu.VMEM((8 * nx, 1, 128), F32),
                    pltpu.VMEM((nz, 1, 128), F32),
-                   dma((NV,)), dma((2,)), dma((NV, 2)), dma((NV, 2)), dma((NV, 2)), dma((NV, 2)),
+                   pltpu.SMEM((2, 4), jnp.int32), pltpu.SMEM((4,), jnp.int32),
+                   dma((NV,)), dma((2,)), dma((2,)),
+                   dma((NV, 2)), dma((NV, 2)), dma((NV, 2)), dma((NV, 2)),
                    dma((NV,)), dma((NV,)), dma((NV, 3)), dma((NV, 3)),
-                   dma((3,)), dma((3,)), pltpu.SemaphoreType.REGULAR((3,))]),
+                   dma((2,)), dma((2,)), pltpu.SemaphoreType.REGULAR((3,))]),
             compiler_params=pltpu.CompilerParams(
                 collective_id=0, has_side_effects=True, vmem_limit_bytes=56 << 20),
         )(dims.T, offsets, vectors, left_env, right_env)
-        return prod, row[0, :9].reshape(3, 3)
+        return pl.pallas_call(
+            hand_over,
+            out_shape=(jax.ShapeDtypeStruct((NV, 4, 32, 256), BF16), jax.ShapeDtypeStruct((3, 3), F32)),
+            in_specs=[vmem, vmem],
+            out_specs=(vmem, vmem),
+            compiler_params=pltpu.CompilerParams(vmem_limit_bytes=2 << 20),
+        )(prod, sub)
 
     return jax.shard_map(
         body,

time: 49.3 us -> 44.3 us (0.90)
  local copies, waits for them, and re-layouts: 2.96 us -> 0 us
  Pallas kernels: 45.5 us -> 43.6 us
    pallas_call x1 -> x2, Pallas kernels: 45.5 us -> 43.6 us  [the longest x1 42.9 us: body(): pl.pallas_call(make_kernel(nz, nx), out_shape=(pltpu.VMEM((NV, 4, 32, 256...]
    unnamed x1 -> x0, local copies, waits for them, and re-layouts: 1.62 us -> none
    slice x1 -> x0, local copies, waits for them, and re-layouts: 0.68 us -> none  [body(): return (prod, row[0, :9].reshape(3, 3))]
    another operation x1 -> x0, local copies, waits for them, and re-layouts: 0.66 us -> none  [body(): return (prod, row[0, :9].reshape(3, 3))]
where the time goes in v2:
time: 44.3 us; the launch traced here: 44.2 us
  Pallas kernels  43.6 us (98%)
  between operations  0.64 us (1%)
    pallas_call x1, Pallas kernels, body(): pl.pallas_call(make_kernel(nz, nx), out_shape=(pltpu.VMEM((NV, 4, 32, 256...  42.9 us

profile of v2, /device:TPU:1, one launch (start us, length us, event | category | flops | bytes accessed | tf_op | source)
XLA Modules:
  0.0 44.2 jit_solution(6974083281856579230)
XLA Ops:
  0.6 42.9 %shard_map.68 = (bf16[3,4,32,256]{3,2,1,0:T(8,128)(2,1)S(1)}, f32[3,3]{1,0:T(4,128)S(1)}) custom-call(s32[2,4]{1,0:T(2,128)} %bitcast.1, s32[4]{0:T(128)} %offsets_hbm.1, bf16[3,4,256,256]{3,2,1,0:T(8,128)(2,1)} %vectors.1, bf16[4,4,256,256]{3,2,1,0:T(8,128)(2,1)} %lenv.1, bf16[4,4,256,256]{3,2,1,0:T(8,128)(2,1)} %renv.1), custom_call_target="tpu_custom_call" | custom-call | tf_op jit(solution)/shard_map/pallas_call | solution.py:246
  43.5 0.7 %shard_map.69 = (bf16[3,4,32,256]{3,2,1,0:T(8,128)(2,1)}, f32[3,3]{1,0:T(4,128)}) custom-call(bf16[3,4,32,256]{3,2,1,0:T(8,128)(2,1)S(1)} %get-tuple-element.4.prod_in, f32[3,3]{1,0:T(4,128)S(1)} %get-tuple-element.5.sub_in), custom_call_target="tpu_custom_call" | custom-call | tf_op jit(solution)/shard_map/pallas_call | solution.py:268

commit v3 on v2

--- a/solution.py
+++ b/solution.py
@@ -21,7 +21,7 @@
     def kernel(dims_hbm, offsets_hbm, vectors, lenv, renv, prod, sub,
                ext0, ext1, ext2, part0, part1, part2, lbuf, rbuf,
                sibrx, ysrc, yrx, ar1, ar3, dims, offsets,
-               vec_sem, env_sem, int_sem, zs_sem, zr_sem, fs_sem, fr_sem, ss_sem, sr_sem, ys_sem, yr_sem,
+               vec_sem, env_sem, int_sem, zs_sem, zr_sem, hs_sem, hr_sem, fs_sem, fr_sem, ss_sem, sr_sem, ys_sem, yr_sem,
                as_sem, a_sem, relay):
         ext = (ext0, ext1, ext2)
         part = (part0, part1, part2)
@@ -69,12 +69,10 @@
         offs_cp.start()
         vec_cp = [pltpu.make_async_copy(vectors.at[v], ext[v].at[pl.ds(2, 4)], vec_sem.at[v])
                   for v in range(NV)]
-        for cp in vec_cp:
-            cp.start()
+        for v in (1, 0, 2):
+            vec_cp[v].start()
         renv_cp = pltpu.make_async_copy(renv, rbuf, env_sem.at[0])
         lenv_cp = pltpu.make_async_copy(lenv, lbuf, env_sem.at[1])
-        renv_cp.start()
-        lenv_cp.start()
 
         dims_cp.wait()
         offs_cp.wait()
@@ -84,20 +82,34 @@
         for s in range(4):
             inside = (row_id < dims[0, s]) & (col_id < dims[1, s])
             masks.append(jnp.where(inside, 1.0, 0.0).astype(BF16))
-        for v in range(NV):
+        def masked(v):
             vec_cp[v].wait()
             for s in range(4):
                 ext[v][2 + s] = ext[v][2 + s] * masks[s]
+
+        masked(1)
         pl.semaphore_wait(barrier, len(near))
 
-        up, down = [], []
-        for v in range(NV):
-            a = remote(ext[v].at[4 + c], ext[v].at[c], zs_sem.at[v, 0], zr_sem.at[v, 0], k, nxt)
-            b = remote(ext[v].at[2 + c], ext[v].at[6 + c], zs_sem.at[v, 1], zr_sem.at[v, 1], k, prv)
-            a.start()
-            b.start()
-            up.append(a)
-            down.append(b)
+        def quarter(v, sector, yy):
+            return ext[v].at[sector, pl.ds(pl.multiple_of(64 * yy, 64), 64)]
+
+        def ahead(n, src, dst):
+            cps = [remote(src(4 + c), dst(c), zs_sem.at[n, 0], zr_sem.at[n, 0], k, nxt),
+                   remote(src(2 + c), dst(6 + c), zs_sem.at[n, 1], zr_sem.at[n, 1], k, prv)]
+            for cp in cps:
+                cp.start()
+            return cps
+
+        opp = lax.rem(y + 2, 4)
+        z_own = ahead(3, lambda e: quarter(1, e, y), lambda e: quarter(1, e, y))
+        masked(0)
+        z_cp = {0: ahead(0, lambda e: ext[0].at[e], lambda e: ext[0].at[e])}
+        z_cp[1] = ahead(1, lambda e: quarter(1, e, opp), lambda e: quarter(1, e, opp))
+        masked(2)
+        z_cp[2] = ahead(2, lambda e: ext[2].at[e], lambda e: ext[2].at[e])
+
+        renv_cp.start()
+        lenv_cp.start()
 
         chain = [beside,
                  [(sib, g), (ypeer(2), g), (k, x_peer(2)), (k, zpeer(2)), (k, zpeer(-2))],
@@ -132,21 +144,35 @@
                 cp.start()
                 y_cp.append(cp)
 
+        hear(0)
+        tell(1)
+        for cp in z_own:
+            cp.wait_recv()
+        h_cp = []
+        for side, sector in enumerate((c, 6 + c)):
+            for way, d in enumerate((1, -1)):
+                cp = remote(quarter(1, sector, y), quarter(1, sector, y), hs_sem.at[side, way],
+                            hr_sem.at[side, way], ypeer(d), g)
+                cp.start()
+                h_cp.append(cp)
+
         accs = {}
-        for v in range(NV):
-            if v >= 1:
-                chip_sum(v - 1)
-            if v == 0:
-                hear(0)
-                tell(1)
-            up[v].wait_recv()
-            down[v].wait_recv()
-            fa = remote(ext[v].at[c], ext[v].at[c], fs_sem.at[v, 0], fr_sem.at[v, 0], sib, g)
-            fb = remote(ext[v].at[6 + c], ext[v].at[6 + c], fs_sem.at[v, 1], fr_sem.at[v, 1], sib, g)
-            fa.start()
-            fb.start()
-            fa.wait()
-            fb.wait()
+        passing = {}
+
+        def pass_on(v):
+            for cp in z_cp[v] + (h_cp if v == 1 else []):
+                cp.wait_recv()
+            passing[v] = [remote(ext[v].at[c], ext[v].at[c], fs_sem.at[v, 0], fr_sem.at[v, 0], sib, g),
+                          remote(ext[v].at[6 + c], ext[v].at[6 + c], fs_sem.at[v, 1], fr_sem.at[v, 1], sib, g)]
+            for cp in passing[v]:
+                cp.start()
+
+        def complete(v):
+            for cp in passing[v]:
+                cp.wait()
+            if v == 1:
+                for cp in h_cp:
+                    cp.wait_send()
 
             @pl.when(g == 0)
             def _():
@@ -156,10 +182,8 @@
             def _():
                 ext[v][6:8] = jnp.zeros((2, 256, 256), BF16)
 
-            if v == 0:
-                renv_cp.wait()
-                lenv_cp.wait()
-            for s in range(4):
+        def products(v, sectors):
+            for s in sectors:
                 tot = None
                 for t in range(4):
                     inner = dot_nt(ext[v][2 + s - offsets[t]], rbuf[t, s]).astype(BF16)
@@ -171,10 +195,26 @@
                     z = jnp.sum(z.reshape(32, 8, 256), axis=0)
                     z = z[:, :128] + z[:, 128:]
                     accs[i, v] = z if s == 0 else accs[i, v] + z
-            sib_send(v)
-            if v == 0:
-                hear(1)
-                tell(2)
+
+        pass_on(0)
+        renv_cp.wait()
+        lenv_cp.wait()
+        complete(0)
+        products(0, (0, 1))
+        pass_on(1)
+        products(0, (2, 3))
+        sib_send(0)
+        hear(1)
+        tell(2)
+        complete(1)
+        products(1, (0, 1))
+        pass_on(2)
+        products(1, (2, 3))
+        sib_send(1)
+        chip_sum(0)
+        complete(2)
+        products(2, (0, 1, 2, 3))
+        sib_send(2)
 
         rows = jnp.concatenate(
             [jnp.sum(accs[i, j], axis=0, keepdims=True) for i in range(NV) for j in range(NV)], axis=0)
@@ -195,6 +235,7 @@
         plane = sorted(((dx, dk) for dx in range(nx) for dk in range(8) if dx + dk),
                        key=lambda p: -(min(p[0], nx - p[0]) + min(p[1] // 2, 4 - p[1] // 2)))
         spread(ar1, 0, [(8 * dx + dk, (term_peer(dk), x_peer(dx))) for dx, dk in plane])
+        chip_sum(1)
         chip_sum(2)
         others(ar1, a_sem.at[0]).wait()
         ar3[0] = jnp.sum(ar1[...], axis=0)
@@ -212,9 +253,8 @@
                     tot = tot + yrx[v, d, s].astype(F32)
                 inside = (rown < dims[0, s]) & (lane < dims[1, s])
                 prod[v, s] = jnp.where(inside, tot, 0.0).astype(BF16)
-        for v in range(NV):
-            up[v].wait_send()
-            down[v].wait_send()
+        for cp in z_own + z_cp[0] + z_cp[1] + z_cp[2]:
+            cp.wait_send()
         others(ar1, as_sem.at[0]).wait()
         others(ar3, as_sem.at[1]).wait()
         others(ar3, a_sem.at[1]).wait()
@@ -259,7 +299,7 @@
                    pltpu.VMEM((nz, 1, 128), F32),
                    pltpu.SMEM((2, 4), jnp.int32), pltpu.SMEM((4,), jnp.int32),
                    dma((NV,)), dma((2,)), dma((2,)),
-                   dma((NV, 2)), dma((NV, 2)), dma((NV, 2)), dma((NV, 2)),
+                   dma((4, 2)), dma((4, 2)), dma((2, 2)), dma((2, 2)), dma((NV, 2)), dma((NV, 2)),
                    dma((NV,)), dma((NV,)), dma((NV, 3)), dma((NV, 3)),
                    dma((2,)), dma((2,)), pltpu.SemaphoreType.REGULAR((3,))]),
             compiler_params=pltpu.CompilerParams(

time: 44.3 us -> 41.3 us (0.932)
  Pallas kernels: 43.6 us -> 40.5 us
    pallas_call x1, Pallas kernels: 42.9 us -> 39.8 us  [body(): pl.pallas_call(make_kernel(nz, nx), out_shape=(pltpu.VMEM((NV, 4, 32, 256...]
where the time goes in v3:
time: 41.3 us; the launch traced here: 41.2 us
  Pallas kernels  40.5 us (98%)
  between operations  0.64 us (2%)
    pallas_call x1, Pallas kernels, body(): pl.pallas_call(make_kernel(nz, nx), out_shape=(pltpu.VMEM((NV, 4, 32, 256...  39.8 us

profile of v3, /device:TPU:1, one launch (start us, length us, event | category | flops | bytes accessed | tf_op | source)
XLA Modules:
  0.0 41.2 jit_solution(4566209545616881358)
XLA Ops:
  0.6 39.8 %shard_map.68 = (bf16[3,4,32,256]{3,2,1,0:T(8,128)(2,1)S(1)}, f32[3,3]{1,0:T(4,128)S(1)}) custom-call(s32[2,4]{1,0:T(2,128)} %bitcast.1, s32[4]{0:T(128)} %offsets_hbm.1, bf16[3,4,256,256]{3,2,1,0:T(8,128)(2,1)} %vectors.1, bf16[4,4,256,256]{3,2,1,0:T(8,128)(2,1)} %lenv.1, bf16[4,4,256,256]{3,2,1,0:T(8,128)(2,1)} %renv.1), custom_call_target="tpu_custom_call" | custom-call | tf_op jit(solution)/shard_map/pallas_call | solution.py:286
  40.5 0.7 %shard_map.69 = (bf16[3,4,32,256]{3,2,1,0:T(8,128)(2,1)}, f32[3,3]{1,0:T(4,128)}) custom-call(bf16[3,4,32,256]{3,2,1,0:T(8,128)(2,1)S(1)} %get-tuple-element.4.prod_in, f32[3,3]{1,0:T(4,128)S(1)} %get-tuple-element.5.sub_in), custom_call_target="tpu_custom_call" | custom-call | tf_op jit(solution)/shard_map/pallas_call | solution.py:308

commit v4 on v3

--- a/solution.py
+++ b/solution.py
@@ -197,6 +197,8 @@
                     accs[i, v] = z if s == 0 else accs[i, v] + z
 
         pass_on(0)
+        hear(1)
+        tell(2)
         renv_cp.wait()
         lenv_cp.wait()
         complete(0)
@@ -204,8 +206,6 @@
         pass_on(1)
         products(0, (2, 3))
         sib_send(0)
-        hear(1)
-        tell(2)
         complete(1)
         products(1, (0, 1))
         pass_on(2)
@@ -270,9 +270,12 @@
     return kernel
 
 
-def hand_over(prod_in, sub_in, prod, sub):
-    prod[...] = prod_in[...]
-    sub[...] = sub_in[...]
+def hand_over(prod_in, sub_in, prod, sub, sem):
+    cps = [pltpu.make_async_copy(prod_in, prod, sem.at[0]), pltpu.make_async_copy(sub_in, sub, sem.at[1])]
+    for cp in cps:
+        cp.start()
+    for cp in cps:
+        cp.wait()
 
 
 def solution(mesh):
@@ -309,7 +312,8 @@
             hand_over,
             out_shape=(jax.ShapeDtypeStruct((NV, 4, 32, 256), BF16), jax.ShapeDtypeStruct((3, 3), F32)),
             in_specs=[vmem, vmem],
-            out_specs=(vmem, vmem),
+            out_specs=(hbm, hbm),
+            scratch_shapes=[dma((2,))],
             compiler_params=pltpu.CompilerParams(vmem_limit_bytes=2 << 20),
         )(prod, sub)
 

time: 41.3 us -> 41.3 us (level)
  no operation moved by 1% of the time
where the time goes in v4:
time: 41.3 us; the launch traced here: 41.2 us
  Pallas kernels  40.5 us (98%)
  between operations  0.64 us (2%)
    pallas_call x1, Pallas kernels, body(): pl.pallas_call(make_kernel(nz, nx), out_shape=(pltpu.VMEM((NV, 4, 32, 256...  39.8 us

profile of v4, /device:TPU:1, one launch (start us, length us, event | category | flops | bytes accessed | tf_op | source)
XLA Modules:
  0.0 41.2 jit_solution(4645204348190201632)
XLA Ops:
  0.6 39.8 %shard_map.68 = (bf16[3,4,32,256]{3,2,1,0:T(8,128)(2,1)S(1)}, f32[3,3]{1,0:T(4,128)S(1)}) custom-call(s32[2,4]{1,0:T(2,128)} %bitcast.1, s32[4]{0:T(128)} %offsets_hbm.1, bf16[3,4,256,256]{3,2,1,0:T(8,128)(2,1)} %vectors.1, bf16[4,4,256,256]{3,2,1,0:T(8,128)(2,1)} %lenv.1, bf16[4,4,256,256]{3,2,1,0:T(8,128)(2,1)} %renv.1), custom_call_target="tpu_custom_call" | custom-call | tf_op jit(solution)/shard_map/pallas_call | solution.py:289
  40.5 0.7 %shard_map.69 = (bf16[3,4,32,256]{3,2,1,0:T(8,128)(2,1)}, f32[3,3]{1,0:T(4,128)}) custom-call(bf16[3,4,32,256]{3,2,1,0:T(8,128)(2,1)S(1)} %get-tuple-element.4.prod_in, f32[3,3]{1,0:T(4,128)S(1)} %get-tuple-element.5.sub_in), custom_call_target="tpu_custom_call" | custom-call | tf_op jit(solution)/shard_map/pallas_call | solution.py:311
